TPU v7x, 128 devices: a whole 4x4x4 slice. The times are simulated.
128 devices in a mesh: src: 16 (over x, z_lo, core), dst: 8 (over z_hi, y).
Axes of the slice: x: 4, y: 4, z: 4 (z_hi: 2, z_lo: 2; z = z_hi * 2 + z_lo), core: 2. Of those that a mesh axis runs over, the one named last changes fastest.
Arguments:
- features: bfloat16 [32768, 1024], P(('src', 'dst')), may hold values from -28 to 28, as said below
- w_src: bfloat16 [1024, 512], replicated, may hold values from -0.1875 to 0.1875
- w_dst: bfloat16 [1024, 512], replicated, may hold values from -0.1875 to 0.1875
- attn: float32 [8, 64], replicated, may hold values from -3 to 3
- bias: float32 [512], replicated, may hold values from -3 to 3
- tile_masks: int32 [16, 8, 16, 8, 128], P('src', 'dst'), may hold values from 0 to 65535, as said below
- tile_dst: int32 [16, 8, 16], P('src', 'dst'), may hold values from 0 to 15, as said below
- tile_src: int32 [16, 8, 16], P('src', 'dst'), may hold values from 0 to 31, as said below
- tile_count: int32 [16, 8], P('src', 'dst'), may hold values from 12 to 16, as said below
Outputs:
- attended: bfloat16 [32768, 512], P(('src', 'dst'))
Inputs may be any that keep to these rules, and one draw needn't show every extreme that they name: Every vertex's features lie within the stated range. `tile_masks`: packed edge bits, 16 source columns a word. `tile_dst`: within one grid block the slots name distinct destination tiles. `tile_src`: within one grid block the slots name distinct source tiles. `tile_count`: some grid block uses all 16 slots.
All inputs are finite; a program needn't handle non-finite values.
Results may differ from a plain program's by a relative error of at most 0.0092.
The roundings to bfloat16 on the way count: a program that leaves them out, or rounds other values in their place, can miss the bound.
Values may be sent and summed in bfloat16 or wider, within the bound.
A program may use at most 64 MiB of HBM per device.

v0:
```python
import jax
import jax.numpy as jnp
from jax import lax
from jax.sharding import PartitionSpec as P

slope = 0.2
floor_value = -1e30


def unpack_edges(words):
    shifts = jnp.arange(16, dtype=jnp.int32)
    bits = words[:, None, :] >> shifts[None, :, None] & 1
    return bits.reshape(128, 128).T > 0


def tile_logits(src_tile, dst_tile, attn):
    heads = attn.shape[0]
    left = src_tile.astype(jnp.float32).reshape(128, heads, -1)
    right = dst_tile.astype(jnp.float32).reshape(128, heads, -1)

    def one_head(index):
        src_part = lax.dynamic_index_in_dim(left, index, 1, keepdims=False)
        dst_part = lax.dynamic_index_in_dim(right, index, 1, keepdims=False)
        weight = lax.dynamic_index_in_dim(attn, index, 0, keepdims=False)
        joined = dst_part[:, None, :] + src_part[None, :, :]
        joined = jnp.where(joined > 0, joined, slope * joined)
        return jnp.sum(joined * weight, axis=-1)

    return lax.map(one_head, jnp.arange(heads, dtype=jnp.int32))


def self_logits(own_l, own_r, attn):
    heads = attn.shape[0]
    joined = own_l.astype(jnp.float32).reshape(own_l.shape[0], heads, -1) + own_r.astype(
        jnp.float32
    ).reshape(own_r.shape[0], heads, -1)
    joined = jnp.where(joined > 0, joined, slope * joined)
    return jnp.sum(joined * attn, axis=-1)


def block_partial(xl_blk, xr_blk, attn, masks, tile_dst, tile_src, count):
    heads = attn.shape[0]
    tiles = masks.shape[0]
    rows = xr_blk.shape[0]
    width = xr_blk.shape[1]

    def first(t, carry):
        logits, best = carry
        src_tile = lax.dynamic_slice_in_dim(xl_blk, tile_src[t] * 128, 128, 0)
        dst_tile = lax.dynamic_slice_in_dim(xr_blk, tile_dst[t] * 128, 128, 0)
        edges = unpack_edges(lax.dynamic_index_in_dim(masks, t, 0, keepdims=False))
        score = jnp.where(edges[None], tile_logits(src_tile, dst_tile, attn), floor_value)
        logits = lax.dynamic_update_index_in_dim(logits, score, t, 0)
        start = tile_dst[t] * 128
        old = lax.dynamic_slice_in_dim(best, start, 128, 0)
        best = lax.dynamic_update_slice_in_dim(
            best, jnp.maximum(old, jnp.max(score, axis=2).T), start, 0
        )
        return (logits, best)

    logits = jnp.full((tiles, heads, 128, 128), floor_value, jnp.float32)
    best = jnp.full((rows, heads), floor_value, jnp.float32)
    logits, best = lax.fori_loop(jnp.int32(0), count, first, (logits, best))

    def second(t, carry):
        total, weight_sum = carry
        start = tile_dst[t] * 128
        edges = unpack_edges(lax.dynamic_index_in_dim(masks, t, 0, keepdims=False))
        top = lax.dynamic_slice_in_dim(best, start, 128, 0).T
        score = lax.dynamic_index_in_dim(logits, t, 0, keepdims=False)
        prob = jnp.where(edges[None], jnp.exp(score - top[:, :, None]), 0.0).astype(jnp.bfloat16)
        src_tile = lax.dynamic_slice_in_dim(xl_blk, tile_src[t] * 128, 128, 0).reshape(
            128, heads, -1
        )
        part = jnp.einsum(
            "hds,shc->dhc", prob, src_tile, preferred_element_type=jnp.float32
        ).reshape(128, width)
        old = lax.dynamic_slice_in_dim(total, start, 128, 0)
        total = lax.dynamic_update_slice_in_dim(total, old + part, start, 0)
        old_sum = lax.dynamic_slice_in_dim(weight_sum, start, 128, 0)
        weight_sum = lax.dynamic_update_slice_in_dim(
            weight_sum, old_sum + jnp.sum(prob.astype(jnp.float32), axis=2).T, start, 0
        )
        return (total, weight_sum)

    total = jnp.zeros((rows, width), jnp.float32)
    weight_sum = jnp.zeros((rows, heads), jnp.float32)
    total, weight_sum = lax.fori_loop(jnp.int32(0), count, second, (total, weight_sum))
    return (best, total, weight_sum)


def body(features, w_src, w_dst, attn, bias, tile_masks, tile_dst, tile_src, tile_count):
    rows = features.shape[0]
    heads = attn.shape[0]
    width = w_src.shape[1]
    own_r = jnp.dot(features, w_dst, preferred_element_type=jnp.float32).astype(jnp.bfloat16)
    xl_blk = jnp.dot(
        lax.all_gather(features, "src", axis=0, tiled=True),
        w_src,
        preferred_element_type=jnp.float32,
    ).astype(jnp.bfloat16)
    own_l = lax.dynamic_slice_in_dim(xl_blk, lax.axis_index("src") * rows, rows, 0)
    xr_blk = lax.all_gather(own_r, "dst", axis=0, tiled=True)
    best, total, weight_sum = block_partial(
        xl_blk, xr_blk, attn, tile_masks[0, 0], tile_dst[0, 0], tile_src[0, 0], tile_count[0, 0]
    )
    self_score = self_logits(own_l, own_r, attn)
    own_start = lax.axis_index("dst") * rows
    lifted = jnp.maximum(lax.dynamic_slice_in_dim(best, own_start, rows, 0), self_score)
    lifted = lax.dynamic_update_slice_in_dim(best, lifted, own_start, 0)
    top = lax.pmax(lifted.astype(jnp.bfloat16), "dst").astype(lifted.dtype)
    scale = jnp.exp(best - top)
    terms = (total.reshape(best.shape[0], heads, -1) * scale[:, :, None]).reshape(
        best.shape[0], width
    )
    summed_total, summed_weight = (
        lax.psum_scatter(terms, "dst", scatter_dimension=0, tiled=True),
        lax.psum_scatter(weight_sum * scale, "dst", scatter_dimension=0, tiled=True),
    )
    own_top = lax.dynamic_slice_in_dim(top, own_start, rows, 0)
    self_weight = jnp.exp(self_score - own_top)
    values = own_l.astype(jnp.float32).reshape(rows, heads, -1) * self_weight[
        :, :, None
    ] + summed_total.reshape(rows, heads, -1)
    denom = self_weight + summed_weight
    return ((values / denom[:, :, None]).reshape(rows, width) + bias).astype(jnp.bfloat16)


def solution(mesh):
    return jax.shard_map(
        body,
        mesh=mesh,
        in_specs=(
            P(("src", "dst"), None),
            P(),
            P(),
            P(),
            P(),
            P("src", "dst", None, None, None),
            P("src", "dst", None),
            P("src", "dst", None),
            P("src", "dst"),
        ),
        out_specs=P(("src", "dst"), None),
        check_vma=False,
    )
```

profile of v0, /device:TPU:1, one launch (start us, length us, event | category | flops | bytes accessed | tf_op | source)
XLA Modules:
  0.0 1147.9 jit_solution(4620975118036065094)
XLA Ops:
  7.3 57.5 %all-gather.3.cloned.1.call-done = bf16[4096,1024]{1,0:T(8,128)(2,1)} async-done(((bf16[256,1024]{1,0:T(8,128)(2,1)}), bf16[4096,1024]{1,0:T(8,128)(2,1)}) %all-gather.3.cloned.1.call-update) | async-done | bytes 8388624 | tf_op jit(solution)/shard_map/all_gather | solution.py:98
  64.9 8.2 convolution_convert_fusion
  73.1 1.8 fusion.18
  75.3 57.3 %all-gather.5.cloned.1.call-done = bf16[2048,512]{0,1:T(8,128)(2,1)} async-done(((bf16[256,512]{0,1:T(8,128)(2,1)}), bf16[2048,512]{0,1:T(8,128)(2,1)}) %all-gather.5.cloned.1.call-update) | async-done | bytes 2097168 | tf_op jit(solution)/shard_map/all_gather | solution.py:103
  132.6 4.3 broadcast_in_dim.55
  136.9 527.3 %while.35 = (s32[]{:T(128)}, f32[16,8,128,128]{3,2,1,0:T(8,128)}, f32[2048,8]{0,1:T(8,128)S(1)}, s32[]{:T(128)}, s32[16,8,128]{2,1,0:T(8,128)}, /*index=5*/s32[1...) while((s32[]{:T(128)}, f32[16,8,128,128]{3,2,1,0:T(8,128)}, ...), condition=%wide.region_6.7_spmd, body=%wide.region_1.6_spmd.sunk | while | flops 6848530 | bytes 3456362 | solution.py:63
  141.1 34.2 %while.37 = (s32[]{:T(128)}, f32[8,128,128]{2,1,0:T(8,128)S(1)}, s32[8]{0:T(128)S(1)}, f32[128,8,64]{0,2,1:T(8,128)S(1)}, f32[128,8,64]{0,2,1:T(8,128)S(1)}, /*i...) while((s32[]{:T(128)}, f32[8,128,128]{2,1,0:T(8,128)S(1)}, s32[8]{0:T(128)S(1)}, ...), condition=%wide.region_4.4_spmd, body=%wide.region_2.3_spmd.sunk | while | flops 6275077 | bytes 459675 | solution.py:29
  143.7 1.6 fusion.44
  156.5 1.6 fusion.44
  160.8 1.6 fusion.44
  165.1 1.6 fusion.44
  169.3 1.6 fusion.44
  173.6 1.6 fusion.44
  181.6 34.2 %while.37 = (s32[]{:T(128)}, f32[8,128,128]{2,1,0:T(8,128)S(1)}, s32[8]{0:T(128)S(1)}, f32[128,8,64]{0,2,1:T(8,128)S(1)}, f32[128,8,64]{0,2,1:T(8,128)S(1)}, /*i...) while((s32[]{:T(128)}, f32[8,128,128]{2,1,0:T(8,128)S(1)}, s32[8]{0:T(128)S(1)}, ...), condition=%wide.region_4.4_spmd, body=%wide.region_2.3_spmd.sunk | while | flops 6275077 | bytes 459675 | solution.py:29
  184.2 1.6 fusion.44
  188.5 1.6 fusion.44
  192.7 1.6 fusion.44
  197.0 1.6 fusion.44
  201.3 1.6 fusion.44
  222.1 34.2 %while.37 = (s32[]{:T(128)}, f32[8,128,128]{2,1,0:T(8,128)S(1)}, s32[8]{0:T(128)S(1)}, f32[128,8,64]{0,2,1:T(8,128)S(1)}, f32[128,8,64]{0,2,1:T(8,128)S(1)}, /*i...) while((s32[]{:T(128)}, f32[8,128,128]{2,1,0:T(8,128)S(1)}, s32[8]{0:T(128)S(1)}, ...), condition=%wide.region_4.4_spmd, body=%wide.region_2.3_spmd.sunk | while | flops 6275077 | bytes 459675 | solution.py:29
  224.7 1.6 fusion.44
  229.0 1.6 fusion.44
  233.2 1.6 fusion.44
  237.5 1.6 fusion.44
  254.6 1.6 fusion.44
  262.6 34.2 %while.37 = (s32[]{:T(128)}, f32[8,128,128]{2,1,0:T(8,128)S(1)}, s32[8]{0:T(128)S(1)}, f32[128,8,64]{0,2,1:T(8,128)S(1)}, f32[128,8,64]{0,2,1:T(8,128)S(1)}, /*i...) while((s32[]{:T(128)}, f32[8,128,128]{2,1,0:T(8,128)S(1)}, s32[8]{0:T(128)S(1)}, ...), condition=%wide.region_4.4_spmd, body=%wide.region_2.3_spmd.sunk | while | flops 6275077 | bytes 459675 | solution.py:29
  265.2 1.6 fusion.44
  269.5 1.6 fusion.44
  282.3 1.6 fusion.44
  286.6 1.6 fusion.44
  290.9 1.6 fusion.44
  295.1 1.6 fusion.44
  303.1 34.2 %while.37 = (s32[]{:T(128)}, f32[8,128,128]{2,1,0:T(8,128)S(1)}, s32[8]{0:T(128)S(1)}, f32[128,8,64]{0,2,1:T(8,128)S(1)}, f32[128,8,64]{0,2,1:T(8,128)S(1)}, /*i...) while((s32[]{:T(128)}, f32[8,128,128]{2,1,0:T(8,128)S(1)}, s32[8]{0:T(128)S(1)}, ...), condition=%wide.region_4.4_spmd, body=%wide.region_2.3_spmd.sunk | while | flops 6275077 | bytes 459675 | solution.py:29
  305.7 1.6 fusion.44
  310.0 1.6 fusion.44
  314.3 1.6 fusion.44
  318.5 1.6 fusion.44
  343.6 34.2 %while.37 = (s32[]{:T(128)}, f32[8,128,128]{2,1,0:T(8,128)S(1)}, s32[8]{0:T(128)S(1)}, f32[128,8,64]{0,2,1:T(8,128)S(1)}, f32[128,8,64]{0,2,1:T(8,128)S(1)}, /*i...) while((s32[]{:T(128)}, f32[8,128,128]{2,1,0:T(8,128)S(1)}, s32[8]{0:T(128)S(1)}, ...), condition=%wide.region_4.4_spmd, body=%wide.region_2.3_spmd.sunk | while | flops 6275077 | bytes 459675 | solution.py:29
  384.1 34.2 %while.37 = (s32[]{:T(128)}, f32[8,128,128]{2,1,0:T(8,128)S(1)}, s32[8]{0:T(128)S(1)}, f32[128,8,64]{0,2,1:T(8,128)S(1)}, f32[128,8,64]{0,2,1:T(8,128)S(1)}, /*i...) while((s32[]{:T(128)}, f32[8,128,128]{2,1,0:T(8,128)S(1)}, s32[8]{0:T(128)S(1)}, ...), condition=%wide.region_4.4_spmd, body=%wide.region_2.3_spmd.sunk | while | flops 6275077 | bytes 459675 | solution.py:29
  424.7 34.2 %while.37 = (s32[]{:T(128)}, f32[8,128,128]{2,1,0:T(8,128)S(1)}, s32[8]{0:T(128)S(1)}, f32[128,8,64]{0,2,1:T(8,128)S(1)}, f32[128,8,64]{0,2,1:T(8,128)S(1)}, /*i...) while((s32[]{:T(128)}, f32[8,128,128]{2,1,0:T(8,128)S(1)}, s32[8]{0:T(128)S(1)}, ...), condition=%wide.region_4.4_spmd, body=%wide.region_2.3_spmd.sunk | while | flops 6275077 | bytes 459675 | solution.py:29
  465.2 34.2 %while.37 = (s32[]{:T(128)}, f32[8,128,128]{2,1,0:T(8,128)S(1)}, s32[8]{0:T(128)S(1)}, f32[128,8,64]{0,2,1:T(8,128)S(1)}, f32[128,8,64]{0,2,1:T(8,128)S(1)}, /*i...) while((s32[]{:T(128)}, f32[8,128,128]{2,1,0:T(8,128)S(1)}, s32[8]{0:T(128)S(1)}, ...), condition=%wide.region_4.4_spmd, body=%wide.region_2.3_spmd.sunk | while | flops 6275077 | bytes 459675 | solution.py:29
  505.7 34.2 %while.37 = (s32[]{:T(128)}, f32[8,128,128]{2,1,0:T(8,128)S(1)}, s32[8]{0:T(128)S(1)}, f32[128,8,64]{0,2,1:T(8,128)S(1)}, f32[128,8,64]{0,2,1:T(8,128)S(1)}, /*i...) while((s32[]{:T(128)}, f32[8,128,128]{2,1,0:T(8,128)S(1)}, s32[8]{0:T(128)S(1)}, ...), condition=%wide.region_4.4_spmd, body=%wide.region_2.3_spmd.sunk | while | flops 6275077 | bytes 459675 | solution.py:29
  546.2 34.2 %while.37 = (s32[]{:T(128)}, f32[8,128,128]{2,1,0:T(8,128)S(1)}, s32[8]{0:T(128)S(1)}, f32[128,8,64]{0,2,1:T(8,128)S(1)}, f32[128,8,64]{0,2,1:T(8,128)S(1)}, /*i...) while((s32[]{:T(128)}, f32[8,128,128]{2,1,0:T(8,128)S(1)}, s32[8]{0:T(128)S(1)}, ...), condition=%wide.region_4.4_spmd, body=%wide.region_2.3_spmd.sunk | while | flops 6275077 | bytes 459675 | solution.py:29
  586.7 34.2 %while.37 = (s32[]{:T(128)}, f32[8,128,128]{2,1,0:T(8,128)S(1)}, s32[8]{0:T(128)S(1)}, f32[128,8,64]{0,2,1:T(8,128)S(1)}, f32[128,8,64]{0,2,1:T(8,128)S(1)}, /*i...) while((s32[]{:T(128)}, f32[8,128,128]{2,1,0:T(8,128)S(1)}, s32[8]{0:T(128)S(1)}, ...), condition=%wide.region_4.4_spmd, body=%wide.region_2.3_spmd.sunk | while | flops 6275077 | bytes 459675 | solution.py:29
  627.2 34.2 %while.37 = (s32[]{:T(128)}, f32[8,128,128]{2,1,0:T(8,128)S(1)}, s32[8]{0:T(128)S(1)}, f32[128,8,64]{0,2,1:T(8,128)S(1)}, f32[128,8,64]{0,2,1:T(8,128)S(1)}, /*i...) while((s32[]{:T(128)}, f32[8,128,128]{2,1,0:T(8,128)S(1)}, s32[8]{0:T(128)S(1)}, ...), condition=%wide.region_4.4_spmd, body=%wide.region_2.3_spmd.sunk | while | flops 6275077 | bytes 459675 | solution.py:29
  664.2 2.5 broadcast_in_dim.57
  666.7 126.5 %while.36 = (s32[]{:T(128)}, f32[2048,512]{0,1:T(8,128)}, f32[2048,8]{0,1:T(8,128)S(1)}, s32[]{:T(128)}, s32[16]{0:T(128)S(1)}, /*index=5*/s32[16]{0:T(128)S(1)}...) while((s32[]{:T(128)}, f32[2048,512]{0,1:T(8,128)}, ...), condition=%wide.region_10.11_spmd, body=%wide.region_8.10_spmd.sunk | while | flops 17940492 | bytes 2619719 | solution.py:88
  673.2 1.7 constant_dynamic-update-slice_fusion.2
  682.8 1.7 constant_dynamic-update-slice_fusion.2
  692.5 1.7 constant_dynamic-update-slice_fusion.2
  702.2 1.7 constant_dynamic-update-slice_fusion.2
  711.9 1.7 constant_dynamic-update-slice_fusion.2
  721.6 1.7 constant_dynamic-update-slice_fusion.2
  731.2 1.7 constant_dynamic-update-slice_fusion.2
  740.9 1.7 constant_dynamic-update-slice_fusion.2
  750.6 1.7 constant_dynamic-update-slice_fusion.2
  760.3 1.7 constant_dynamic-update-slice_fusion.2
  770.0 1.7 constant_dynamic-update-slice_fusion.2
  779.7 1.7 constant_dynamic-update-slice_fusion.2
  789.3 1.7 constant_dynamic-update-slice_fusion.2
  793.2 176.9 %pmax.7 = bf16[2048,8]{0,1:T(8,128)(2,1)S(1)} all-reduce(bf16[2048,8]{0,1:T(8,128)(2,1)S(1)} %convert_element_type.34), channel_id=1, replica_groups=mesh['src'=16,'dst'=8] {'dst'}, use_global_device_ids=true, to_apply=%region_7.8 | all-reduce | flops 16384 | bytes 65536 | tf_op jit(solution)/shard_map/pmax | solution.py:111
  970.8 4.7 bitcast_multiply_fusion
  975.6 75.1 %reduce-scatter.5.cloned.1.call-done = f32[256,8]{0,1:T(8,128)} async-done(((f32[2048,8]{0,1:T(8,128)}), f32[256,8]{0,1:T(8,128)}) %reduce-scatter.5.cloned.1.call-update) | async-done | bytes 8208 | tf_op jit(solution)/shard_map/reduce_scatter | solution.py:118
  1051.4 87.9 %reduce-scatter.3.cloned.1.call-done = f32[256,512]{0,1:T(8,128)} async-done(((f32[2048,512]{0,1:T(8,128)}), f32[256,512]{0,1:T(8,128)}) %reduce-scatter.3.cloned.1.call-update) | async-done | bytes 524304 | tf_op jit(solution)/shard_map/reduce_scatter | solution.py:117
  (1087 shorter events, 344.7 us)
Async XLA Ops:
  6.5 58.4 %copy-start = (bf16[1024,512]{1,0:T(8,128)(2,1)S(1)}, bf16[1024,512]{1,0:T(8,128)(2,1)}, u32[]{:S(2)}) copy-start(bf16[1024,512]{1,0:T(8,128)(2,1)} %param.16) | copy-start | bytes 3145732
  6.5 58.4 %all-gather.3.cloned.1.call-start = ((), (), s32[]{:S(2)}) async-start(), calls=%async_computation.2 | async-start | bytes 8912896 | tf_op jit(solution)/shard_map/all_gather | solution.py:98
  7.3 125.3 %all-gather.5.cloned.1.call-start = ((), (), s32[]{:S(2)}) async-start(), calls=%async_computation.3 | async-start | bytes 2359296 | tf_op jit(solution)/shard_map/all_gather | solution.py:103
  7.3 65.8 %copy-start.1 = (bf16[256,1024]{1,0:T(8,128)(2,1)S(1)}, bf16[256,1024]{1,0:T(8,128)(2,1)}, u32[]{:S(2)}) copy-start(bf16[256,1024]{1,0:T(8,128)(2,1)} %param.15) | copy-start | bytes 1572868
  7.3 65.8 %copy-start.2 = (bf16[1024,512]{1,0:T(8,128)(2,1)S(1)}, bf16[1024,512]{1,0:T(8,128)(2,1)}, u32[]{:S(2)}) copy-start(bf16[1024,512]{1,0:T(8,128)(2,1)} %param.17) | copy-start | bytes 3145732
  7.3 65.8 %copy-start.4 = (f32[8,64]{1,0:T(8,128)S(1)}, f32[8,64]{1,0:T(8,128)}, u32[]{:S(2)}) copy-start(f32[8,64]{1,0:T(8,128)} %param.18) | copy-start | bytes 6148
  73.1 2.1 copy-start.3
  75.2 975.4 %reduce-scatter.5.cloned.1.call-start = ((), (), s32[]{:S(2)}) async-start(), calls=%async_computation.5 | async-start | bytes 73728 | tf_op jit(solution)/shard_map/reduce_scatter | solution.py:118
  132.6 4.3 copy-start.6
  132.6 4.3 copy-start.7
  970.7 168.5 %reduce-scatter.3.cloned.1.call-start = ((), (), s32[]{:S(2)}) async-start(), calls=%async_computation.4 | async-start | bytes 4718592 | tf_op jit(solution)/shard_map/reduce_scatter | solution.py:117
  975.5 163.7 %copy-start.5 = (f32[512]{0:T(512)S(1)}, f32[512]{0:T(512)}, u32[]{:S(2)}) copy-start(f32[512]{0:T(512)} %param.19) | copy-start | bytes 6148
Sparse Core Ops, SparseCore 0:
  9.1 55.7 all-gather.2
  75.4 57.1 all-gather.4
  970.8 79.7 reduce-scatter.4
  1054.4 84.8 reduce-scatter.2
where the time goes:
time: 1160 us; the launch traced here: 1150 us
  waiting for transfers between devices  279 us (24%)
  loops' own time  249 us (21%)
  other arithmetic  237 us (20%)
  blocking collectives  177 us (15%)
  local copies, waits for them, and re-layouts  165 us (14%)
  matrix products  28.3 us (2%)
  between operations  13.3 us (1%)
    another operation x13, loops' own time, tile_logits(): return lax.map(one_head, jnp.arange(heads, dtype=jnp.int32))  196 us
    pmax x1, blocking collectives, body(): top = lax.pmax(lifted.astype(jnp.bfloat16), 'dst').astype(lifted.dtype)  177 us
    reduce_sum x104, other arithmetic, one_head(): return jnp.sum(joined * weight, axis=-1)  171 us
    reduce_scatter x1, waiting for transfers between devices, body(): lax.psum_scatter(terms, 'dst', scatter_dimension=0, tiled=True)  87.9 us
    reduce_scatter x1, waiting for transfers between devices, body(): lax.psum_scatter(weight_sum * scale, 'dst', scatter_dimension=0, tiled=True)  75.1 us
    dynamic_slice x104, local copies, waits for them, and re-layouts, tile_logits(): return lax.map(one_head, jnp.arange(heads, dtype=jnp.int32))  63.9 us
    all_gather x1, waiting for transfers between devices, body(): lax.all_gather(features, 'src', axis=0, tiled=True)  57.5 us
    all_gather x1, waiting for transfers between devices, body(): xr_blk = lax.all_gather(own_r, 'dst', axis=0, tiled=True)  57.3 us
  transfers between devices with their start and end apart: 4, of which 4 were waited for; matrix products, arithmetic and copies ran while one was open for 0% of the time, Pallas kernels for 0%

commit v1 on v0

v1 whole, which is shorter than its diff:
```python
import functools

import jax
import jax.numpy as jnp
from jax import lax
from jax.experimental import pallas as pl
from jax.experimental.pallas import tpu as pltpu
from jax.sharding import PartitionSpec as P

f32, bf16, i32 = jnp.float32, jnp.bfloat16, jnp.int32
MESH = pl.DeviceIdType.MESH
TILE = 128
FLOOR = -1e30
HALF_FLOOR = -5e29


def nt(a, b):
    return lax.dot_general(a, b, (((1,), (1,)), ((), ())), preferred_element_type=f32)


def mm(a, b):
    return jnp.dot(a, b, preferred_element_type=f32)


def split(x):
    hi = x.astype(bf16)
    return hi, (x - hi.astype(f32)).astype(bf16)


def iota(shape, dim):
    return lax.broadcasted_iota(i32, shape, dim)


def make_coefficients(attn_ref, alin_ref, aw_ref, brep_ref):
    attn = attn_ref[...]
    tiled = jnp.concatenate([attn] * 8, 1)
    diag = jnp.where(iota((8, 512), 0) == iota((8, 512), 1) // 64, tiled, 0.0)
    flat = jnp.sum(diag, axis=0, keepdims=True)
    same = iota((TILE, TILE), 0) // 64 == iota((TILE, TILE), 1) // 64
    for hp in range(4):
        row = jnp.broadcast_to(flat[:, hp * TILE : (hp + 1) * TILE], (TILE, TILE))
        rep = jnp.where(same, row.T, 0.0)
        parts = split(rep) + split(-0.8 * rep)
        for k, part in enumerate(parts):
            brep_ref[hp, :, k * TILE : (k + 1) * TILE] = part
    k4 = iota((8, TILE), 0) % 4
    half = iota((8, TILE), 1) // 64
    for st in range(2):
        fv = jnp.broadcast_to(flat[:, st * TILE : (st + 1) * TILE], (8, TILE))
        fw = jnp.broadcast_to(flat[:, (st + 2) * TILE : (st + 3) * TILE], (8, TILE))
        lin = jnp.concatenate(
            [jnp.where(k4 == half, fv, 0.0), jnp.where(k4 - 2 == half, fw, 0.0)], 1
        )
        hi, lo = split(lin)
        alin_ref[st] = jnp.concatenate([hi, lo], 0)
        both = -0.8 * jnp.concatenate(
            [jnp.where(k4 == half, fw, 0.0), jnp.where(k4 - 2 == half, fw, 0.0)], 1
        )
        hi, lo = split(both)
        aw_ref[st] = jnp.concatenate([hi, lo], 0)


def prepare_self(st, nu_ref, own_ref, brep_ref, num_ref, den_ref, top_ref):
    for k in range(2):
        ls = slice(k * TILE, (k + 1) * TILE)
        v = own_ref[st, :, ls]
        w = jnp.minimum(nu_ref[st, :, ls].astype(bf16), v)
        b = brep_ref[st + 2 * k]
        top_ref[2 * st + k] = (
            mm(v, b[:, :128]) + mm(v, b[:, 128:256]) + mm(w, b[:, 256:384]) + mm(w, b[:, 384:])
        )
        num_ref[2 * st + k] = v.astype(f32)
        den_ref[2 * st + k] = jnp.ones((256, TILE), f32)


def logits_step(st, dtile, step, nuv_ref, nu_ref, xs_ref, vt_ref, attn_sm, aw_ref, e_ref):
    block = step // 2
    h2 = step % 2
    i0 = pl.multiple_of(dtile * TILE + block * 16, 16)
    ublk = nuv_ref[h2, pl.ds(i0, 16), :]
    i8 = pl.multiple_of(dtile * TILE + block * 16 + h2 * 8, 8)
    rows8 = nu_ref[st, pl.ds(i8, 8), TILE:]
    aw = aw_ref[st]
    low = iota((8, TILE), 0) < 4

    def matrix_piece(quad, g):
        xsw = xs_ref[st, 2 * g + dtile, :, TILE:]
        halves = []
        for a in range(2):
            parts = []
            for b in range(2):
                r = quad * 4 + a * 2 + b
                rb = jnp.broadcast_to(rows8[r : r + 1], (16, TILE)).astype(bf16)
                parts.append(jnp.minimum(jnp.tile(rb, (8, 1)), xsw))
            halves.append(jnp.concatenate(parts, 1))
        res = nt(aw, jnp.concatenate(halves, 0))
        res = res[:8] + res[8:16]
        at = pl.multiple_of(block * 32 + h2 * 16 + quad * 8, 8)
        e_ref[g, 1, pl.ds(at, 8), :] = jnp.where(low, res[:, :TILE], res[:, TILE:])

    pieces = [(q, g) for q in range(2) for g in range(8)]
    done = 0
    acc = [jnp.zeros((16, TILE), f32) for _ in range(8)]
    for c in range(64):
        ub = jnp.broadcast_to(ublk[:, c : c + 1], (16, TILE))
        co = attn_sm[st * 2 + h2, c]
        for g in range(8):
            vb = vt_ref[2 * g + dtile, pl.ds(h2 * 64 + c, 1), :]
            acc[g] = acc[g] + co * jnp.minimum(ub, vb)
        while done < (c + 1) * len(pieces) // 64:
            matrix_piece(*pieces[done])
            done += 1
    for g in range(8):
        e_ref[g, 0, pl.ds(block * 32 + h2, 16, stride=2), :] = -0.8 * acc[g]


def mask_bias(words):
    parts = jnp.concatenate([words & 255, (words >> 8) & 255], 0).astype(f32).astype(bf16)
    k = iota((16, TILE), 0)
    pick = ((k % 8) * 2 + k // 8 == iota((16, TILE), 1) // 8).astype(f32).astype(bf16)
    spread = lax.dot_general(parts, pick, (((0,), (0,)), ((), ())), preferred_element_type=f32)
    bits = spread.astype(i32) & (1 << (iota((TILE, TILE), 1) % 8))
    return jnp.where(bits != 0, 0.0, FLOOR)


def finish_step(st, dtile, step, xs_ref, floor_ref, lin_ref, e_ref, num_ref, den_ref, top_ref):
    g = step // 2
    pair = step % 2
    u = 2 * g + dtile
    even = iota((TILE, TILE), 1) < 64
    evenb = even.astype(f32).astype(bf16)
    oddb = (1 - even.astype(f32)).astype(bf16)
    bias = floor_ref[u]
    ps, ms = [], []
    for h2 in range(2):
        e = e_ref[g, pair, pl.ds(h2, TILE, stride=2), :]
        s = e + (lin_ref[st, u, pl.ds(pair * 2 + h2, 1), :] + bias)
        m = jnp.max(s, axis=1, keepdims=True)
        ps.append(jnp.exp(s - jnp.maximum(m, HALF_FLOOR)).astype(bf16))
        ms.append(m)
    p = jnp.concatenate(ps, 1)
    xp = xs_ref[st, u, :, pl.ds(pl.multiple_of(pair * TILE, TILE), TILE)]
    wt = jnp.concatenate(
        [jnp.concatenate([xp * evenb, evenb], 1), jnp.concatenate([xp * oddb, oddb], 1)], 0
    )
    us = mm(p, wt)
    m = jnp.where(even, ms[0], ms[1])
    at = (2 * st + pair, slice(dtile * TILE, (dtile + 1) * TILE), slice(None))
    old = top_ref[at]
    top = jnp.maximum(old, m)
    a = jnp.exp(old - top)
    b = jnp.exp(m - top)
    top_ref[at] = top
    num_ref[at] = num_ref[at] * a + us[:, :TILE] * b
    den_ref[at] = den_ref[at] * a + us[:, TILE:] * b


def kernel(
    feat_hbm, wsrc_hbm, wdst_hbm, attn_hbm, bias_hbm, mask_hbm, tdst_hbm, tsrc_hbm, count_hbm,
    out_ref,
    feat, wsrc, wdst, attn, bias, mask, attn_sm, tdst, tsrc, tcount, load_sem,
    xg0, xg1, stage, mstage, xs, mk, nu, nuv, own, vt, ea, eb, num, den, top, alin, aw, brep,
    floor_ref, lin, table, gsend, grecv, asend, arecv, msend, mrecv,
):
    s = lax.axis_index("src")
    d = lax.axis_index("dst")
    x, zl, core = s // 4, (s // 2) % 2, s % 2
    zh, y = d // 4, d % 4

    def at(xx, zz, cc):
        return lax.rem(xx + 4, 4) * 4 + zz * 2 + cc

    sib = at(x, zl, 1 - core)
    zn = at(x, 1 - zl, core)
    xp = at(x + 1, zl, core)
    xm = at(x - 1, zl, core)
    dest = [lax.rem(zh + r // 4, 2) * 4 + lax.rem(y + r % 4, 4) for r in range(8)]

    loads = []

    def load(src, dst):
        copy = pltpu.make_async_copy(src, dst, load_sem.at[len(loads)])
        copy.start()
        loads.append(copy)

    def columns(ref, k):
        return ref.at[:, pl.ds(k * TILE, TILE)]

    load(feat_hbm, feat)
    for st in range(2):
        for k in range(2):
            load(columns(wsrc_hbm, st + 2 * k), wsrc.at[st, :, pl.ds(k * TILE, TILE)])
    load(tdst_hbm, tdst)
    load(tsrc_hbm, tsrc)
    load(count_hbm, tcount)
    load(mask_hbm, mask)
    for st in range(2):
        for k in range(2):
            load(columns(wdst_hbm, st + 2 * k), wdst.at[st, :, pl.ds(k * TILE, TILE)])
    load(attn_hbm, attn)
    load(attn_hbm, attn_sm)
    load(bias_hbm, bias)

    barrier = pltpu.get_barrier_semaphore()
    partners = [(p, d) for p in (sib, zn, xp, xm)] + [(s, dest[r]) for r in range(1, 8)]
    for partner in partners:
        pl.semaphore_signal(barrier, inc=1, device_id=partner, device_id_type=MESH)

    xg = (xg0, xg1)
    copies = []

    def send(st, slot, part, to):
        ref = xg[st].at[slot] if part is None else xg[st].at[slot, part]
        copy = pltpu.make_async_remote_copy(
            src_ref=ref,
            dst_ref=ref,
            send_sem=gsend.at[len(copies)],
            recv_sem=grecv.at[st, slot, part or 0],
            device_id=(to, d),
            device_id_type=MESH,
        )
        copy.start()
        copies.append(copy)

    def arrived(st, slot, part=None):
        ref = xg[st].at[slot] if part is None else xg[st].at[slot, part]
        pltpu.make_async_remote_copy(
            src_ref=ref,
            dst_ref=ref,
            send_sem=gsend.at[0],
            recv_sem=grecv.at[st, slot, part or 0],
            device_id=(sib, d),
            device_id_type=MESH,
        ).wait_recv()

    def project(st):
        xl = mm(feat[...], wsrc[st]).astype(bf16)
        own[st] = xl
        xg[st][s] = xl.reshape(2, TILE, 256)

    for copy in loads[:3]:
        copy.wait()
    project(0)
    pl.semaphore_wait(barrier, len(partners))
    for to in (zn, xp, xm, sib):
        send(0, s, None, to)
    for copy in loads[3:5]:
        copy.wait()
    project(1)
    send(1, s, None, zn)

    for copy in loads[5:9]:
        copy.wait()

    def fill(t_dst, _):
        src, slot, used = jnp.int32(0), jnp.int32(0), jnp.int32(0)
        for t in range(16):
            hit = jnp.where((tdst[t] == t_dst) & (t < tcount[0, 0]), 1, 0)
            src, slot, used = src + hit * tsrc[t], slot + hit * t, used + hit
        table[0, t_dst] = src
        table[1, t_dst] = slot
        table[2, t_dst] = used
        return 0

    lax.fori_loop(0, 16, fill, 0)
    mask_copies = []
    for r in range(8):
        for k in range(2):
            tile = dest[r] * 2 + k
            words = mask[table[1, tile]] * table[2, tile]
            if r == 0:
                mk[k] = words
            else:
                mstage[r * 2 + k] = words
        if r:
            copy = pltpu.make_async_remote_copy(
                src_ref=mstage.at[pl.ds(r * 2, 2)],
                dst_ref=mk.at[pl.ds(r * 2, 2)],
                send_sem=msend.at[r],
                recv_sem=mrecv.at[r],
                device_id=(s, dest[r]),
                device_id_type=MESH,
            )
            copy.start()
            mask_copies.append(copy)

    def relay_plane(st):
        arrived(st, zn)
        for to in (xp, xm, sib):
            send(st, zn, None, to)

    def relay_near(st, z):
        left, right = at(x - 1, z, core), at(x + 1, z, core)
        arrived(st, left)
        send(st, left, 0, xp)
        send(st, left, None, sib)
        arrived(st, right)
        send(st, right, 1, xm)
        send(st, right, None, sib)

    def relay_far(st):
        for z in (zl, 1 - zl):
            for part in range(2):
                arrived(st, at(x + 2, z, core), part)
                send(st, at(x + 2, z, core), part, sib)

    def siblings(st):
        for z in (zl, 1 - zl):
            for dx in (0, 1, -1):
                arrived(st, at(x + dx, z, 1 - core))
        for z in (zl, 1 - zl):
            for part in range(2):
                arrived(st, at(x + 2, z, 1 - core), part)

    tile_copies = [[], []]

    def exchange(st):
        for r in (4, 6, 5, 7, 2, 1, 3, 0):
            for k in range(2):
                src = table[0, dest[r] * 2 + k]
                tile = xg[st][src // 2, src % 2]
                if r == 0:
                    xs[st, k] = tile
                else:
                    stage[st, r * 2 + k] = tile
            if r:
                copy = pltpu.make_async_remote_copy(
                    src_ref=stage.at[st, pl.ds(r * 2, 2)],
                    dst_ref=xs.at[st, pl.ds(r * 2, 2)],
                    send_sem=asend.at[st, r],
                    recv_sem=arecv.at[st, r],
                    device_id=(s, dest[r]),
                    device_id_type=MESH,
                )
                copy.start()
                tile_copies[st].append(copy)

    def project_dst(st):
        nu[st] = -mm(feat[...], wdst[st]).astype(bf16).astype(f32)

    relay_plane(0)
    relay_near(0, zl)
    for copy in loads[9:]:
        copy.wait()
    relay_near(0, 1 - zl)
    for to in (xp, xm, sib):
        send(1, s, None, to)
    relay_plane(1)
    project_dst(0)
    relay_far(0)
    siblings(0)
    exchange(0)
    relay_near(1, zl)
    project_dst(1)
    relay_near(1, 1 - zl)
    make_coefficients(attn, alin, aw, brep)
    for st in range(2):
        prepare_self(st, nu, own, brep, num, den, top)
    relay_far(1)
    for copy in mask_copies:
        copy.wait_recv()

    def floors(u, _):
        floor_ref[u] = mask_bias(mk[u])
        return 0

    lax.fori_loop(0, 16, floors, 0)
    siblings(1)
    exchange(1)

    def begin(st):
        for copy in tile_copies[st]:
            copy.wait_recv()
        for h2 in range(2):
            part = nu[st, :, :TILE]
            nuv[h2] = part if h2 == 0 else pltpu.roll(part, 64, 1)

        def turn(u, _):
            vt[u] = xs[st, u, :, :TILE].astype(f32).T
            res = nt(alin[st], xs[st, u])
            lin[st, u] = res[:8] + res[8:]
            return 0

        lax.fori_loop(0, 16, turn, 0, unroll=4)

    def run(now, before):
        def step(n, _):
            if before is not None:
                finish_step(
                    before[0], before[1], n, xs, floor_ref, lin, before[2], num, den, top
                )
            if now is not None:
                logits_step(now[0], now[1], n, nuv, nu, xs, vt, attn_sm, aw, now[2])
            return 0

        lax.fori_loop(0, 16, step, 0)

    phases = [(0, 0, ea), (0, 1, eb), (1, 0, ea), (1, 1, eb)]
    for k, now in enumerate(phases):
        if k % 2 == 0:
            begin(now[0])
        run(now, phases[k - 1] if k else None)
    run(None, phases[-1])

    for st in range(2):
        for k in range(2):
            q = 2 * st + k
            ls = slice((st + 2 * k) * TILE, (st + 2 * k + 1) * TILE)
            out_ref[:, ls] = (num[q] / den[q] + bias[:, ls]).astype(bf16)
    for copy in copies + mask_copies + tile_copies[0] + tile_copies[1]:
        copy.wait_send()


def body(features, w_src, w_dst, attn, bias, tile_masks, tile_dst, tile_src, tile_count):
    hbm = pl.BlockSpec(memory_space=pl.ANY)
    dma = pltpu.SemaphoreType.DMA
    scratch = [
        pltpu.VMEM((256, 1024), bf16),
        pltpu.VMEM((2, 1024, 256), bf16),
        pltpu.VMEM((2, 1024, 256), bf16),
        pltpu.VMEM((8, 64), f32),
        pltpu.VMEM((1, 512), f32),
        pltpu.VMEM((16, 8, TILE), i32),
        pltpu.SMEM((8, 64), f32),
        pltpu.SMEM((16,), i32),
        pltpu.SMEM((16,), i32),
        pltpu.SMEM((1, 1), i32),
        dma((16,)),
        pltpu.VMEM((16, 2, TILE, 256), bf16),
        pltpu.VMEM((16, 2, TILE, 256), bf16),
        pltpu.VMEM((2, 16, TILE, 256), bf16),
        pltpu.VMEM((16, 8, TILE), i32),
        pltpu.VMEM((2, 16, TILE, 256), bf16),
        pltpu.VMEM((16, 8, TILE), i32),
        pltpu.VMEM((2, 256, 256), f32),
        pltpu.VMEM((2, 256, TILE), f32),
        pltpu.VMEM((2, 256, 256), bf16),
        pltpu.VMEM((16, TILE, TILE), f32),
        pltpu.VMEM((8, 2, 256, TILE), f32),
        pltpu.VMEM((8, 2, 256, TILE), f32),
        pltpu.VMEM((4, 256, TILE), f32),
        pltpu.VMEM((4, 256, TILE), f32),
        pltpu.VMEM((4, 256, TILE), f32),
        pltpu.VMEM((2, 16, 256), bf16),
        pltpu.VMEM((2, 16, 256), bf16),
        pltpu.VMEM((4, TILE, 512), bf16),
        pltpu.VMEM((16, TILE, TILE), f32),
        pltpu.VMEM((2, 16, 8, TILE), f32),
        pltpu.SMEM((3, 16), i32),
        dma((38,)),
        dma((2, 16, 2)),
        dma((2, 8)),
        dma((2, 8)),
        dma((8,)),
        dma((8,)),
    ]
    return pl.pallas_call(
        kernel,
        out_shape=jax.ShapeDtypeStruct((256, 512), bf16),
        in_specs=[hbm] * 9,
        out_specs=pl.BlockSpec(memory_space=pltpu.VMEM),
        scratch_shapes=scratch,
        compiler_params=pltpu.CompilerParams(
            collective_id=0, has_side_effects=True, vmem_limit_bytes=60 * 2**20
        ),
    )(
        features, w_src, w_dst, attn, bias.reshape(1, 512), tile_masks[0, 0],
        tile_dst[0, 0], tile_src[0, 0], tile_count,
    )


def solution(mesh):
    return jax.shard_map(
        body,
        mesh=mesh,
        in_specs=(
            P(("src", "dst"), None),
            P(),
            P(),
            P(),
            P(),
            P("src", "dst", None, None, None),
            P("src", "dst", None),
            P("src", "dst", None),
            P("src", "dst"),
        ),
        out_specs=P(("src", "dst"), None),
        check_vma=False,
    )
```

time: 1160 us -> 114 us (0.10); the launches traced: 1150 us -> 114 us
  waiting for transfers between devices: 279 us -> 0 us
  loops' own time: 249 us -> 0 us
  other arithmetic: 237 us -> 0 us
  blocking collectives: 177 us -> 0 us
  local copies, waits for them, and re-layouts: 165 us -> 1.67 us
  Pallas kernels: 0 us -> 112 us
  matrix products: 28.3 us -> 0 us
  between operations: 13.3 us -> 0.66 us
    another operation x15 -> x0, loops' own time: 249 us -> none  [the longest x13 196 us: tile_logits(): return lax.map(one_head, jnp.arange(heads, dtype=jnp.int32))]
    reduce_sum x117 -> x0, other arithmetic: 190 us -> none  [the longest x104 171 us: one_head(): return jnp.sum(joined * weight, axis=-1)]
    pmax x1 -> x0, blocking collectives: 177 us -> none  [body(): top = lax.pmax(lifted.astype(jnp.bfloat16), 'dst').astype(lifted.dtype)]
    reduce_scatter x2 -> x0, waiting for transfers between devices: 163 us -> none  [the longest x1 87.9 us: body(): lax.psum_scatter(terms, 'dst', scatter_dimension=0, tiled=True)]
    dynamic_slice x390 -> x0, local copies, waits for them, and re-layouts: 131 us -> none  [the longest x104 63.9 us: tile_logits(): return lax.map(one_head, jnp.arange(heads, dtype=jnp.int32))]
    all_gather x2 -> x0, waiting for transfers between devices: 115 us -> none  [the longest x1 57.5 us: body(): lax.all_gather(features, 'src', axis=0, tiled=True)]
    pallas_call x0 -> x1, Pallas kernels: none -> 112 us  [body(): pl.pallas_call(kernel, out_shape=jax.ShapeDtypeStruct((256, 512), bf16),...]
    dynamic_update_slice x53 -> x0, other arithmetic: 33.7 us -> none  [the longest x13 22.2 us: second(): total = lax.dynamic_update_slice_in_dim(total, old + part, start, 0)]
  transfers between devices with their start and end apart: 4 -> 0, of which waited for: 4 -> 0; matrix products, arithmetic and copies ran while one was open for 0% -> 0% of each run, Pallas kernels for 0% -> 0%
where the time goes in v1:
time: 114 us
  Pallas kernels  112 us (98%)
  local copies, waits for them, and re-layouts  1.67 us (1%)
    pallas_call x1, Pallas kernels, body(): pl.pallas_call(kernel, out_shape=jax.ShapeDtypeStruct((256, 512), bf16),...  112 us

profile of v1, /device:TPU:1, one launch (start us, length us, event | category | flops | bytes accessed | tf_op | source)
XLA Modules:
  0.0 114.3 jit_solution(3937491868883682124)
XLA Ops:
  0.7 112.0 %shard_map.91 = bf16[256,512]{1,0:T(8,128)(2,1)} custom-call(bf16[256,1024]{1,0:T(8,128)(2,1)} %feat_hbm.1, bf16[1024,512]{1,0:T(8,128)(2,1)} %wsrc_hbm.1, bf16[1024,512]{1,0:T(8,128)(2,1)} %wdst_hbm.1, f32[8,64]{1,0:T(8,128)} %attn_hbm.1, f32[1,512]{1,0:T(1,128)} %bitcast.5, s32[16,8,128]{2,1,0:T(8,128)} %bitcast.4, s32[16]{0:T(128)} %bitcast.6, ...), custom_call_target="tpu_custom_call" | custom-call | tf_op jit(solution)/shard_map/pallas_call | solution.py:457
  112.6 1.7 %copy.12 = bf16[256,512]{1,0:T(8,128)(2,1)} copy(bf16[256,512]{1,0:T(8,128)(2,1)} %shard_map.91) | data formatting | bytes 524288

commit v2 on v1

--- a/solution.py
+++ b/solution.py
@@ -97,17 +97,22 @@
         res = res[:8] + res[8:16]
         at = pl.multiple_of(block * 32 + h2 * 16 + quad * 8, 8)
         e_ref[g, 1, pl.ds(at, 8), :] = jnp.where(low, res[:, :TILE], res[:, TILE:])
+        tokens.append(res[:, :TILE] * 0.0)
 
     pieces = [(q, g) for q in range(2) for g in range(8)]
     done = 0
+    tokens = []
     acc = [jnp.zeros((16, TILE), f32) for _ in range(8)]
     for c in range(64):
         ub = jnp.broadcast_to(ublk[:, c : c + 1], (16, TILE))
+        k = c // 4 - 2
+        if c % 4 == 0 and 0 <= k < len(tokens):
+            ub = ub + jnp.concatenate([tokens[k]] * 2, 0)
         co = attn_sm[st * 2 + h2, c]
         for g in range(8):
             vb = vt_ref[2 * g + dtile, pl.ds(h2 * 64 + c, 1), :]
             acc[g] = acc[g] + co * jnp.minimum(ub, vb)
-        while done < (c + 1) * len(pieces) // 64:
+        while done < len(pieces) and c >= 4 * done - 12:
             matrix_piece(*pieces[done])
             done += 1
     for g in range(8):
@@ -145,7 +150,7 @@
     )
     us = mm(p, wt)
     m = jnp.where(even, ms[0], ms[1])
-    at = (2 * st + pair, slice(dtile * TILE, (dtile + 1) * TILE), slice(None))
+    at = (2 * st + pair, pl.ds(pl.multiple_of(dtile * TILE, TILE), TILE), slice(None))
     old = top_ref[at]
     top = jnp.maximum(old, m)
     a = jnp.exp(old - top)
@@ -159,7 +164,7 @@
     feat_hbm, wsrc_hbm, wdst_hbm, attn_hbm, bias_hbm, mask_hbm, tdst_hbm, tsrc_hbm, count_hbm,
     out_ref,
     feat, wsrc, wdst, attn, bias, mask, attn_sm, tdst, tsrc, tcount, load_sem,
-    xg0, xg1, stage, mstage, xs, mk, nu, nuv, own, vt, ea, eb, num, den, top, alin, aw, brep,
+    xg0, xg1, stage, mstage, xs, mk, nu, nuv, own, vt, e_ref, num, den, top, alin, aw, brep,
     floor_ref, lin, table, gsend, grecv, asend, arecv, msend, mrecv,
 ):
     s = lax.axis_index("src")
@@ -248,6 +253,68 @@
         copy.wait()
     project(1)
     send(1, s, None, zn)
+
+    def relay_plane(st):
+        arrived(st, zn)
+        for to in (xp, xm, sib):
+            send(st, zn, None, to)
+
+    def relay_near(st, z):
+        left, right = at(x - 1, z, core), at(x + 1, z, core)
+        arrived(st, left)
+        send(st, left, 0, xp)
+        send(st, left, None, sib)
+        arrived(st, right)
+        send(st, right, 1, xm)
+        send(st, right, None, sib)
+
+    def relay_far(st):
+        for z in (zl, 1 - zl):
+            for part in range(2):
+                arrived(st, at(x + 2, z, core), part)
+                send(st, at(x + 2, z, core), part, sib)
+
+    def siblings(st):
+        for z in (zl, 1 - zl):
+            for dx in (0, 1, -1):
+                arrived(st, at(x + dx, z, 1 - core))
+        for z in (zl, 1 - zl):
+            for part in range(2):
+                arrived(st, at(x + 2, z, 1 - core), part)
+
+    tile_copies = {}
+
+    def exchange(st):
+        for k in range(2):
+            for r in (4, 6, 5, 7, 2, 1, 3, 0):
+                src = table[0, dest[r] * 2 + k]
+                tile = xg[st][src // 2, src % 2]
+                if r == 0:
+                    xs[st, k] = tile
+                    continue
+                stage[st, r * 2 + k] = tile
+                copy = pltpu.make_async_remote_copy(
+                    src_ref=stage.at[st, r * 2 + k],
+                    dst_ref=xs.at[st, r * 2 + k],
+                    send_sem=asend.at[st, k, r],
+                    recv_sem=arecv.at[st, k, r],
+                    device_id=(s, dest[r]),
+                    device_id_type=MESH,
+                )
+                copy.start()
+                tile_copies[st, k, r] = copy
+
+    def project_dst(st):
+        nu[st] = -mm(feat[...], wdst[st]).astype(bf16).astype(f32)
+
+    relay_plane(0)
+    relay_near(0, zl)
+    for copy in loads[9:]:
+        copy.wait()
+    relay_near(0, 1 - zl)
+    for to in (xp, xm, sib):
+        send(1, s, None, to)
+    relay_plane(1)
 
     for copy in loads[5:9]:
         copy.wait()
@@ -284,79 +351,16 @@
             copy.start()
             mask_copies.append(copy)
 
-    def relay_plane(st):
-        arrived(st, zn)
-        for to in (xp, xm, sib):
-            send(st, zn, None, to)
-
-    def relay_near(st, z):
-        left, right = at(x - 1, z, core), at(x + 1, z, core)
-        arrived(st, left)
-        send(st, left, 0, xp)
-        send(st, left, None, sib)
-        arrived(st, right)
-        send(st, right, 1, xm)
-        send(st, right, None, sib)
-
-    def relay_far(st):
-        for z in (zl, 1 - zl):
-            for part in range(2):
-                arrived(st, at(x + 2, z, core), part)
-                send(st, at(x + 2, z, core), part, sib)
-
-    def siblings(st):
-        for z in (zl, 1 - zl):
-            for dx in (0, 1, -1):
-                arrived(st, at(x + dx, z, 1 - core))
-        for z in (zl, 1 - zl):
-            for part in range(2):
-                arrived(st, at(x + 2, z, 1 - core), part)
-
-    tile_copies = [[], []]
-
-    def exchange(st):
-        for r in (4, 6, 5, 7, 2, 1, 3, 0):
-            for k in range(2):
-                src = table[0, dest[r] * 2 + k]
-                tile = xg[st][src // 2, src % 2]
-                if r == 0:
-                    xs[st, k] = tile
-                else:
-                    stage[st, r * 2 + k] = tile
-            if r:
-                copy = pltpu.make_async_remote_copy(
-                    src_ref=stage.at[st, pl.ds(r * 2, 2)],
-                    dst_ref=xs.at[st, pl.ds(r * 2, 2)],
-                    send_sem=asend.at[st, r],
-                    recv_sem=arecv.at[st, r],
-                    device_id=(s, dest[r]),
-                    device_id_type=MESH,
-                )
-                copy.start()
-                tile_copies[st].append(copy)
-
-    def project_dst(st):
-        nu[st] = -mm(feat[...], wdst[st]).astype(bf16).astype(f32)
-
-    relay_plane(0)
-    relay_near(0, zl)
-    for copy in loads[9:]:
-        copy.wait()
-    relay_near(0, 1 - zl)
-    for to in (xp, xm, sib):
-        send(1, s, None, to)
-    relay_plane(1)
-    project_dst(0)
     relay_far(0)
     siblings(0)
     exchange(0)
+    project_dst(0)
     relay_near(1, zl)
     project_dst(1)
     relay_near(1, 1 - zl)
     make_coefficients(attn, alin, aw, brep)
     for st in range(2):
         prepare_self(st, nu, own, brep, num, den, top)
-    relay_far(1)
     for copy in mask_copies:
         copy.wait_recv()
 
@@ -364,50 +368,50 @@
         floor_ref[u] = mask_bias(mk[u])
         return 0
 
-    lax.fori_loop(0, 16, floors, 0)
-    siblings(1)
-    exchange(1)
-
-    def begin(st):
-        for copy in tile_copies[st]:
-            copy.wait_recv()
-        for h2 in range(2):
-            part = nu[st, :, :TILE]
-            nuv[h2] = part if h2 == 0 else pltpu.roll(part, 64, 1)
-
-        def turn(u, _):
+    lax.fori_loop(0, 16, floors, 0, unroll=2)
+    relay_far(1)
+
+    def begin(st, dtile):
+        for r in range(1, 8):
+            tile_copies[st, dtile, r].wait_recv()
+        if dtile == 0:
+            for h2 in range(2):
+                part = nu[st, :, :TILE]
+                nuv[h2] = part if h2 == 0 else pltpu.roll(part, 64, 1)
+
+        def turn(g, _):
+            u = 2 * g + dtile
             vt[u] = xs[st, u, :, :TILE].astype(f32).T
             res = nt(alin[st], xs[st, u])
             lin[st, u] = res[:8] + res[8:]
             return 0
 
-        lax.fori_loop(0, 16, turn, 0, unroll=4)
-
-    def run(now, before):
-        def step(n, _):
-            if before is not None:
-                finish_step(
-                    before[0], before[1], n, xs, floor_ref, lin, before[2], num, den, top
-                )
-            if now is not None:
-                logits_step(now[0], now[1], n, nuv, nu, xs, vt, attn_sm, aw, now[2])
-            return 0
-
-        lax.fori_loop(0, 16, step, 0)
-
-    phases = [(0, 0, ea), (0, 1, eb), (1, 0, ea), (1, 1, eb)]
-    for k, now in enumerate(phases):
-        if k % 2 == 0:
-            begin(now[0])
-        run(now, phases[k - 1] if k else None)
-    run(None, phases[-1])
+        lax.fori_loop(0, 8, turn, 0, unroll=4)
+
+    for st in range(2):
+        for dtile in range(2):
+            if (st, dtile) == (0, 1):
+                siblings(1)
+                exchange(1)
+            begin(st, dtile)
+
+            def step(n, _):
+                logits_step(st, dtile, n, nuv, nu, xs, vt, attn_sm, aw, e_ref)
+                return 0
+
+            def finish(n, _):
+                finish_step(st, dtile, n, xs, floor_ref, lin, e_ref, num, den, top)
+                return 0
+
+            lax.fori_loop(0, 16, step, 0, unroll=2)
+            lax.fori_loop(0, 16, finish, 0, unroll=4)
 
     for st in range(2):
         for k in range(2):
             q = 2 * st + k
             ls = slice((st + 2 * k) * TILE, (st + 2 * k + 1) * TILE)
             out_ref[:, ls] = (num[q] / den[q] + bias[:, ls]).astype(bf16)
-    for copy in copies + mask_copies + tile_copies[0] + tile_copies[1]:
+    for copy in copies + mask_copies + list(tile_copies.values()):
         copy.wait_send()
 
 
@@ -437,7 +441,6 @@
         pltpu.VMEM((2, 256, 256), bf16),
         pltpu.VMEM((16, TILE, TILE), f32),
         pltpu.VMEM((8, 2, 256, TILE), f32),
-        pltpu.VMEM((8, 2, 256, TILE), f32),
         pltpu.VMEM((4, 256, TILE), f32),
         pltpu.VMEM((4, 256, TILE), f32),
         pltpu.VMEM((4, 256, TILE), f32),
@@ -449,8 +452,8 @@
         pltpu.SMEM((3, 16), i32),
         dma((38,)),
         dma((2, 16, 2)),
-        dma((2, 8)),
-        dma((2, 8)),
+        dma((2, 2, 8)),
+        dma((2, 2, 8)),
         dma((8,)),
         dma((8,)),
     ]

time: 114 us -> 97.3 us (0.85)
  Pallas kernels: 112 us -> 94.8 us
    pallas_call x1, Pallas kernels: 112 us -> 94.8 us  [body(): pl.pallas_call(kernel, out_shape=jax.ShapeDtypeStruct((256, 512), bf16),...]
where the time goes in v2:
time: 97.3 us; the launch traced here: 97.1 us
  Pallas kernels  94.8 us (97%)
  local copies, waits for them, and re-layouts  1.67 us (2%)
    pallas_call x1, Pallas kernels, body(): pl.pallas_call(kernel, out_shape=jax.ShapeDtypeStruct((256, 512), bf16),...  94.8 us

profile of v2, /device:TPU:1, one launch (start us, length us, event | category | flops | bytes accessed | tf_op | source)
XLA Modules:
  0.0 97.1 jit_solution(10685648503028631796)
XLA Ops:
  0.7 94.8 %shard_map.91 = bf16[256,512]{1,0:T(8,128)(2,1)} custom-call(bf16[256,1024]{1,0:T(8,128)(2,1)} %feat_hbm.1, bf16[1024,512]{1,0:T(8,128)(2,1)} %wsrc_hbm.1, bf16[1024,512]{1,0:T(8,128)(2,1)} %wdst_hbm.1, f32[8,64]{1,0:T(8,128)} %attn_hbm.1, f32[1,512]{1,0:T(1,128)} %bitcast.5, s32[16,8,128]{2,1,0:T(8,128)} %bitcast.4, s32[16]{0:T(128)} %bitcast.6, ...), custom_call_target="tpu_custom_call" | custom-call | tf_op jit(solution)/shard_map/pallas_call | solution.py:460
  95.4 1.7 %copy.12 = bf16[256,512]{1,0:T(8,128)(2,1)} copy(bf16[256,512]{1,0:T(8,128)(2,1)} %shard_map.91) | data formatting | bytes 524288

commit v3 on v2

--- a/solution.py
+++ b/solution.py
@@ -105,7 +105,7 @@
     acc = [jnp.zeros((16, TILE), f32) for _ in range(8)]
     for c in range(64):
         ub = jnp.broadcast_to(ublk[:, c : c + 1], (16, TILE))
-        k = c // 4 - 2
+        k = c // 4 - 1
         if c % 4 == 0 and 0 <= k < len(tokens):
             ub = ub + jnp.concatenate([tokens[k]] * 2, 0)
         co = attn_sm[st * 2 + h2, c]
@@ -404,7 +404,7 @@
                 return 0
 
             lax.fori_loop(0, 16, step, 0, unroll=2)
-            lax.fori_loop(0, 16, finish, 0, unroll=4)
+            lax.fori_loop(0, 16, finish, 0, unroll=8)
 
     for st in range(2):
         for k in range(2):

time: 97.3 us -> 95.6 us (0.983)
  Pallas kernels: 94.8 us -> 93.1 us
    pallas_call x1, Pallas kernels: 94.8 us -> 93.1 us  [body(): pl.pallas_call(kernel, out_shape=jax.ShapeDtypeStruct((256, 512), bf16),...]
where the time goes in v3:
time: 95.6 us; the launch traced here: 95.4 us
  Pallas kernels  93.1 us (97%)
  local copies, waits for them, and re-layouts  1.67 us (2%)
    pallas_call x1, Pallas kernels, body(): pl.pallas_call(kernel, out_shape=jax.ShapeDtypeStruct((256, 512), bf16),...  93.1 us

profile of v3, /device:TPU:1, one launch (start us, length us, event | category | flops | bytes accessed | tf_op | source)
XLA Modules:
  0.0 95.4 jit_solution(5900816236639088440)
XLA Ops:
  0.7 93.1 %shard_map.91 = bf16[256,512]{1,0:T(8,128)(2,1)} custom-call(bf16[256,1024]{1,0:T(8,128)(2,1)} %feat_hbm.1, bf16[1024,512]{1,0:T(8,128)(2,1)} %wsrc_hbm.1, bf16[1024,512]{1,0:T(8,128)(2,1)} %wdst_hbm.1, f32[8,64]{1,0:T(8,128)} %attn_hbm.1, f32[1,512]{1,0:T(1,128)} %bitcast.5, s32[16,8,128]{2,1,0:T(8,128)} %bitcast.4, s32[16]{0:T(128)} %bitcast.6, ...), custom_call_target="tpu_custom_call" | custom-call | tf_op jit(solution)/shard_map/pallas_call | solution.py:460
  93.8 1.7 %copy.12 = bf16[256,512]{1,0:T(8,128)(2,1)} copy(bf16[256,512]{1,0:T(8,128)(2,1)} %shard_map.91) | data formatting | bytes 524288

commit v4 on v3

--- a/solution.py
+++ b/solution.py
@@ -440,7 +440,7 @@
         pltpu.VMEM((2, 256, TILE), f32),
         pltpu.VMEM((2, 256, 256), bf16),
         pltpu.VMEM((16, TILE, TILE), f32),
-        pltpu.VMEM((8, 2, 256, TILE), f32),
+        pltpu.VMEM((8, 2, 264, TILE), f32),
         pltpu.VMEM((4, 256, TILE), f32),
         pltpu.VMEM((4, 256, TILE), f32),
         pltpu.VMEM((4, 256, TILE), f32),

time: 95.6 us -> 95.9 us (level)
  no operation moved by 1% of the time
where the time goes in v4:
time: 95.9 us; the launch traced here: 95.7 us
  Pallas kernels  93.4 us (97%)
  local copies, waits for them, and re-layouts  1.67 us (2%)
    pallas_call x1, Pallas kernels, body(): pl.pallas_call(kernel, out_shape=jax.ShapeDtypeStruct((256, 512), bf16),...  93.4 us

profile of v4, /device:TPU:1, one launch (start us, length us, event | category | flops | bytes accessed | tf_op | source)
XLA Modules:
  0.0 95.7 jit_solution(3211174184068945801)
XLA Ops:
  0.7 93.4 %shard_map.91 = bf16[256,512]{1,0:T(8,128)(2,1)} custom-call(bf16[256,1024]{1,0:T(8,128)(2,1)} %feat_hbm.1, bf16[1024,512]{1,0:T(8,128)(2,1)} %wsrc_hbm.1, bf16[1024,512]{1,0:T(8,128)(2,1)} %wdst_hbm.1, f32[8,64]{1,0:T(8,128)} %attn_hbm.1, f32[1,512]{1,0:T(1,128)} %bitcast.5, s32[16,8,128]{2,1,0:T(8,128)} %bitcast.4, s32[16]{0:T(128)} %bitcast.6, ...), custom_call_target="tpu_custom_call" | custom-call | tf_op jit(solution)/shard_map/pallas_call | solution.py:460
  94.0 1.7 %copy.12 = bf16[256,512]{1,0:T(8,128)(2,1)} copy(bf16[256,512]{1,0:T(8,128)(2,1)} %shard_map.91) | data formatting | bytes 524288
